TPU v7x, 32 devices: a whole 2x2x4 slice. The times are simulated.
32 devices in a mesh: dp: 8 (over z, y), tensor: 4 (over x, core).
Axes of the slice: x: 2, y: 2, z: 4, core: 2. Of those that a mesh axis runs over, the one named last changes fastest.
Arguments:
- inputs: bfloat16 [2048, 6144], P('dp', 'tensor'), may hold values from -250 to 250
- upstream: bfloat16 [2048, 1024], P('dp', 'tensor'), may hold values from -6 to 6
- proj_weight: bfloat16 [6144, 1024], P(None, 'tensor'), may hold values from -0.078125 to 0.078125
- proj_bias: float32 [1024], P('tensor'), may hold values from -4 to 4
- norm_gain: float32 [6144], replicated, may hold values from 0.1 to 1.9
- home_rows: int32 [2048], P('dp'), may hold values from 0 to 2047, as said below
Outputs:
- home_grad: bfloat16 [2048, 6144], P('dp', 'tensor')
Inputs may be any that keep to these rules, and one draw needn't show every extreme that they name: `home_rows`: A permutation of 0 to 2047. The balanced row at position i * 256 + k goes to a home row j * 256 + s (0 <= s < 256); of the 256 rows of one dp index, at most 64 have the same owner j, and in every draw some do.
All inputs are finite; a program needn't handle non-finite values.
Results may differ from a plain program's by a relative error of at most 0.018.
Values may be sent and summed in bfloat16 or wider, within the bound.
A program may use at most 64 MiB of HBM per device.

v0:
```python
import jax
import jax.numpy as jnp
from jax import lax
from jax.sharding import PartitionSpec as P

epsilon = 1e-05


def contract_cols(left, right):
    return lax.dot_general(
        left, right, (((1,), (1,)), ((), ())), preferred_element_type=jnp.float32
    )


def per_device(inputs, upstream, proj_weight, proj_bias, norm_gain, home_rows):
    gathered = lax.all_gather(inputs, "tensor", axis=1, tiled=True).astype(jnp.float32)
    row_mean = jnp.mean(gathered, axis=1, keepdims=True)
    centred = gathered - row_mean
    inv_std = lax.rsqrt(jnp.mean(centred * centred, axis=1, keepdims=True) + epsilon)
    unit_rows = centred * inv_std
    normed = (unit_rows * norm_gain[None, :]).astype(jnp.bfloat16)
    preact = jnp.dot(normed, proj_weight, preferred_element_type=jnp.float32) + proj_bias[None, :]
    gate_value = jax.nn.sigmoid(preact)
    pre_grad = (
        upstream.astype(jnp.float32) * gate_value * (1.0 + preact * (1.0 - gate_value))
    ).astype(jnp.bfloat16)
    row_total = upstream.shape[0]
    block_rows = row_total // lax.axis_size("tensor")
    first_row = lax.axis_index("tensor") * block_rows
    mine = lax.psum_scatter(
        contract_cols(pre_grad, proj_weight).astype(jnp.bfloat16),
        "tensor",
        scatter_dimension=0,
        tiled=True,
    ).astype(jnp.float32)
    own_unit = lax.dynamic_slice_in_dim(unit_rows, first_row, block_rows, 0)
    own_scale = lax.dynamic_slice_in_dim(inv_std, first_row, block_rows, 0)
    scaled = mine * norm_gain[None, :]
    input_grad = (
        own_scale
        * (
            scaled
            - jnp.mean(scaled, axis=1, keepdims=True)
            - own_unit * jnp.mean(scaled * own_unit, axis=1, keepdims=True)
        )
    ).astype(jnp.bfloat16)
    column_rows = lax.all_to_all(input_grad, "tensor", split_axis=1, concat_axis=0, tiled=True)
    owners = lax.axis_size("dp")
    capacity = max(2, 2 * row_total // owners)
    owner_of = home_rows // row_total
    home_slot = home_rows % row_total
    order_ids = jnp.arange(row_total, dtype=jnp.int32)
    earlier = jnp.sum(
        (
            (owner_of[:, None] == owner_of[None, :]) & (order_ids[:, None] > order_ids[None, :])
        ).astype(jnp.int32),
        axis=1,
    )
    target = owner_of * capacity + earlier
    placing = jnp.arange(owners * capacity, dtype=jnp.int32)[:, None] == target[None, :]
    send_rows = jnp.dot(
        placing.astype(jnp.bfloat16), column_rows, preferred_element_type=jnp.float32
    ).astype(jnp.bfloat16)
    send_slots = (jnp.sum(jnp.where(placing, home_slot[None, :] + 1, 0), axis=1) - 1)[:, None]
    arrived, arrived_slots = (
        lax.all_to_all(send_rows, "dp", split_axis=0, concat_axis=0, tiled=True),
        lax.all_to_all(send_slots, "dp", split_axis=0, concat_axis=0, tiled=True),
    )
    landing = order_ids[:, None] == arrived_slots[None, :, 0]
    return jnp.dot(
        landing.astype(jnp.bfloat16), arrived, preferred_element_type=jnp.float32
    ).astype(jnp.bfloat16)


def solution(mesh):
    return jax.shard_map(
        per_device,
        mesh=mesh,
        in_specs=(
            P("dp", "tensor"),
            P("dp", "tensor"),
            P(None, "tensor"),
            P("tensor"),
            P(),
            P("dp"),
        ),
        out_specs=P("dp", "tensor"),
        check_vma=False,
    )
```

profile of v0, /device:TPU:0, one launch (start us, length us, event | category | flops | bytes accessed | tf_op | source)
XLA Modules:
  0.0 172.0 jit_solution(7080336451724407404)
XLA Ops:
  6.5 0.0 copy-start
  6.5 0.0 all-gather.2.cloned.1.call-start
  6.5 0.0 copy-start.2
  6.5 0.0 copy-start.4
  6.5 0.7 all-gather.2.cloned.1.call-update
  7.3 0.0 copy-start.5
  7.3 0.0 reduce-scatter.2.cloned.1.call-start
  7.3 32.9 %all-gather.2.cloned.1.call-done = bf16[256,6144]{1,0:T(8,128)(2,1)} async-done(((bf16[256,1536]{1,0:T(8,128)(2,1)}), bf16[256,6144]{1,0:T(8,128)(2,1)}) %all-gather.2.cloned.1.call-update) | async-done | bytes 3145744 | tf_op jit(solution)/shard_map/all_gather | solution.py:16
  40.2 0.0 copy-start.1
  40.2 2.5 %convert_reduce_fusion = f32[256]{0:T(256)S(1)} fusion(bf16[256,6144]{1,0:T(8,128)(2,1)} %all-gather.2.cloned.1.call-done), kind=kLoop, calls=%fused_computation.1 | loop fusion | flops 3145472 | bytes 3146752 | tf_op jit(solution)/shard_map/reduce_sum | solution.py:17
  42.7 0.3 copy-done.1
  43.0 1.0 fusion.2
  44.0 0.0 copy-done
  44.0 0.0 copy-done.2
  44.0 0.0 copy-done.4
  44.0 0.0 copy-done.5
  44.0 7.1 %convolution_convert_fusion = bf16[256,6144]{1,0:T(8,128)(2,1)} fusion(bf16[6144,256]{1,0:T(8,128)(2,1)S(1)} %copy-done, f32[6144]{0:T(1024)S(1)} %copy-done.2, bf16[256,256]{1,0:T(8,128)(2,1)S(1)} %copy-done.4, f32[256]{0:T(256)S(1)} %copy-done.5, bf16[256,6144]{1,0:T(8,128)(2,1)} %all-gather.2.cloned.1.call-done, f32[256]{0:T(256)S(1)} %add_rsqrt_fusion, ...), kind=kOutput, calls=%fused_computation.2 | convolution fusion | flops 1620770816 | bytes 9595904 | tf_op jit(solution)/shard_map/dot_general | solution.py:10
  51.1 0.0 copy-start.3
  51.1 0.0 reduce-scatter.2.cloned.1.call-update
  51.1 0.6 copy-done.3
  51.8 0.1 dynamic-slice.3
  51.9 5.7 %fusion = f32[256,6144]{1,0:T(8,128)} fusion(bf16[256,6144]{1,0:T(8,128)(2,1)} %all-gather.2.cloned.1.call-done, f32[256]{0:T(256)S(1)} %add_rsqrt_fusion, f32[256]{0:T(256)S(1)} %broadcast_multiply_fusion), kind=kLoop, calls=%fused_computation.3 | loop fusion | flops 4718592 | bytes 9439232 | tf_op jit(solution)/shard_map/mul | solution.py:20
  57.5 31.7 %reduce-scatter.2.cloned.1.call-done = bf16[64,6144]{1,0:T(8,128)(2,1)} async-done(((bf16[256,6144]{1,0:T(8,128)(2,1)}), bf16[64,6144]{1,0:T(8,128)(2,1)}) %reduce-scatter.2.cloned.1.call-update) | async-done | bytes 786448 | tf_op jit(solution)/shard_map/reduce_scatter | solution.py:30
  89.2 2.0 %fusion.5 = (f32[64]{0:T(128)S(1)}, f32[64]{0:T(128)S(1)}) fusion(bf16[64,6144]{1,0:T(8,128)(2,1)} %reduce-scatter.2.cloned.1.call-done, f32[6144]{0:T(1024)S(1)} %copy-done.2, f32[256,6144]{1,0:T(8,128)} %fusion, s32[]{:T(128)S(6)} %select_n.23), kind=kLoop, calls=%fused_computation.14 | loop fusion | flops 1965952 | bytes 2384388 | tf_op jit(solution)/shard_map/reduce_sum | solution.py:43
  91.3 2.0 %multiply_convert_fusion.2 = bf16[64,6144]{1,0:T(8,128)(2,1)S(1)} fusion(bf16[64,6144]{1,0:T(8,128)(2,1)} %reduce-scatter.2.cloned.1.call-done, f32[256,6144]{1,0:T(8,128)} %fusion, s32[]{:T(128)S(6)} %select_n.23, f32[64]{0:T(128)S(1)} %get-tuple-element.9, f32[64]{0:T(128)S(1)} %get-tuple-element.10, f32[6144]{0:T(1024)S(1)} %copy-done.2, ...), kind=kLoop, calls=%fused_computation.11 | loop fusion | flops 2752512 | bytes 3171076 | tf_op jit(solution)/shard_map/convert_element_type | solution.py:46
  93.3 0.9 copy.14
  94.2 4.2 %all-to-all-start.1 = ((bf16[64,4,1536]{2,0,1:T(8,128)(2,1)}), bf16[64,4,1536]{2,0,1:T(8,128)(2,1)}, u32[]{:S(2)}, u32[]{:S(2)}) async-start(bf16[64,4,1536]{2,0,1:T(8,128)(2,1)} %bitcast.16), calls=%async_computation.2 | async-start | bytes 1572864 | tf_op jit(solution)/shard_map/all_to_all | solution.py:47
  98.4 0.2 convert_reduce_fusion.1
  98.6 0.2 select_reduce_fusion
  98.8 0.7 sub.36
  99.5 10.7 %all-to-all-done.1 = bf16[64,4,1536]{2,0,1:T(8,128)(2,1)} async-done(((bf16[64,4,1536]{2,0,1:T(8,128)(2,1)}), bf16[64,4,1536]{2,0,1:T(8,128)(2,1)}, u32[]{:S(2)}, u32[]{:S(2)}) %all-to-all-start.1) | async-done | bytes 786464 | tf_op jit(solution)/shard_map/all_to_all | solution.py:47
  110.1 5.5 %all-to-all-start = ((s32[8,64,1]{1,2,0:T(1,128)}), s32[8,64,1]{1,2,0:T(1,128)S(1)}, u32[]{:S(2)}, u32[]{:S(2)}) async-start(s32[8,64,1]{1,2,0:T(1,128)} %bitcast), calls=%async_computation | async-start | bytes 8192 | tf_op jit(solution)/shard_map/all_to_all | solution.py:67
  115.7 2.9 %convolution_convert_fusion.1 = bf16[512,1536]{1,0:T(8,128)(2,1)} fusion(bf16[256,1536]{1,0:T(8,128)(2,1)} %bitcast.2, s32[256]{0:T(256)S(1)} %multiply_add_fusion), kind=kOutput, calls=%fused_computation.9 | convolution fusion | flops 403570688 | bytes 2360320 | tf_op jit(solution)/shard_map/dot_general | solution.py:61
  118.5 3.6 %all-to-all-done = s32[8,64,1]{1,2,0:T(1,128)S(1)} async-done(((s32[8,64,1]{1,2,0:T(1,128)}), s32[8,64,1]{1,2,0:T(1,128)S(1)}, u32[]{:S(2)}, u32[]{:S(2)}) %all-to-all-start) | async-done | bytes 2080 | tf_op jit(solution)/shard_map/all_to_all | solution.py:67
  122.1 4.3 %all-to-all-start.2 = ((bf16[8,64,1536]{2,1,0:T(8,128)(2,1)}), bf16[8,64,1536]{2,1,0:T(8,128)(2,1)}, u32[]{:S(2)}, u32[]{:S(2)}) async-start(bf16[8,64,1536]{2,1,0:T(8,128)(2,1)} %bitcast.15), calls=%async_computation.3 | async-start | bytes 3145728 | tf_op jit(solution)/shard_map/all_to_all | solution.py:66
  126.4 0.5 broadcast.124
  126.9 0.7 reduce.3
  127.6 0.1 eq.50
  127.7 34.6 %all-to-all-done.2 = bf16[8,64,1536]{2,1,0:T(8,128)(2,1)} async-done(((bf16[8,64,1536]{2,1,0:T(8,128)(2,1)}), bf16[8,64,1536]{2,1,0:T(8,128)(2,1)}, u32[]{:S(2)}, u32[]{:S(2)}) %all-to-all-start.2) | async-done | bytes 1572896 | tf_op jit(solution)/shard_map/all_to_all | solution.py:66
  162.3 2.9 %convolution_convert_fusion.2 = bf16[256,1536]{1,0:T(8,128)(2,1)} fusion(bf16[512,1536]{1,0:T(8,128)(2,1)} %bitcast.4, s32[512]{0:T(512)S(1)} %eq.50), kind=kOutput, calls=%fused_computation.10 | convolution fusion | flops 403177472 | bytes 2361344 | tf_op jit(solution)/shard_map/dot_general | solution.py:70
  (6 shorter events, 0.0 us)
Async XLA Ops:
  6.5 37.5 %copy-start = (bf16[6144,256]{1,0:T(8,128)(2,1)S(1)}, bf16[6144,256]{1,0:T(8,128)(2,1)}, u32[]{:S(2)}) copy-start(bf16[6144,256]{1,0:T(8,128)(2,1)} %param.8) | copy-start | bytes 9437188
  6.5 33.6 %all-gather.2.cloned.1.call-start = ((), (), s32[]{:S(2)}) async-start(), calls=%async_computation.4 | async-start | bytes 3932160 | tf_op jit(solution)/shard_map/all_gather | solution.py:16
  6.5 37.5 %copy-start.2 = (f32[6144]{0:T(1024)S(1)}, f32[6144]{0:T(1024)}, u32[]{:S(2)}) copy-start(f32[6144]{0:T(1024)} %param.10) | copy-start | bytes 73732
  6.5 37.5 %copy-start.4 = (bf16[256,256]{1,0:T(8,128)(2,1)S(1)}, bf16[256,256]{1,0:T(8,128)(2,1)}, u32[]{:S(2)}) copy-start(bf16[256,256]{1,0:T(8,128)(2,1)} %param.7) | copy-start | bytes 393220
  7.3 36.8 %copy-start.5 = (f32[256]{0:T(256)S(1)}, f32[256]{0:T(256)}, u32[]{:S(2)}) copy-start(f32[256]{0:T(256)} %param.9) | copy-start | bytes 3076
  7.3 82.0 %reduce-scatter.2.cloned.1.call-start = ((), (), s32[]{:S(2)}) async-start(), calls=%async_computation.5 | async-start | bytes 3932160 | tf_op jit(solution)/shard_map/reduce_scatter | solution.py:30
  40.2 2.8 %copy-start.1 = (bf16[256,6144]{1,0:T(8,128)(2,1)S(1)}, bf16[256,6144]{1,0:T(8,128)(2,1)}, u32[]{:S(2)}) copy-start(bf16[256,6144]{1,0:T(8,128)(2,1)} %all-gather.2.cloned.1.call-done) | copy-start | bytes 9437188
  51.1 0.7 copy-start.3
  94.2 15.9 %all-to-all-start.1 = ((bf16[64,4,1536]{2,0,1:T(8,128)(2,1)}), bf16[64,4,1536]{2,0,1:T(8,128)(2,1)}, u32[]{:S(2)}, u32[]{:S(2)}) async-start(bf16[64,4,1536]{2,0,1:T(8,128)(2,1)} %bitcast.16), calls=%async_computation.2 | async-start | bytes 1572864 | tf_op jit(solution)/shard_map/all_to_all | solution.py:47
  110.1 12.0 %all-to-all-start = ((s32[8,64,1]{1,2,0:T(1,128)}), s32[8,64,1]{1,2,0:T(1,128)S(1)}, u32[]{:S(2)}, u32[]{:S(2)}) async-start(s32[8,64,1]{1,2,0:T(1,128)} %bitcast), calls=%async_computation | async-start | bytes 8192 | tf_op jit(solution)/shard_map/all_to_all | solution.py:67
  122.1 40.1 %all-to-all-start.2 = ((bf16[8,64,1536]{2,1,0:T(8,128)(2,1)}), bf16[8,64,1536]{2,1,0:T(8,128)(2,1)}, u32[]{:S(2)}, u32[]{:S(2)}) async-start(bf16[8,64,1536]{2,1,0:T(8,128)(2,1)} %bitcast.15), calls=%async_computation.3 | async-start | bytes 3145728 | tf_op jit(solution)/shard_map/all_to_all | solution.py:66
Sparse Core Ops, SparseCore 0:
  8.9 31.2 all-gather.1
  51.2 37.9 reduce-scatter.1
where the time goes:
time: 172 us
  waiting for transfers between devices  114 us (66%)
  other arithmetic  14.3 us (8%)
  starting transfers between devices  14 us (8%)
  between operations  13.5 us (8%)
  matrix products  12.8 us (7%)
  local copies, waits for them, and re-layouts  3.22 us (2%)
    all_to_all x1, waiting for transfers between devices, per_device(): lax.all_to_all(send_rows, 'dp', split_axis=0, concat_axis=0, tiled=True)  34.6 us
    all_gather x1, waiting for transfers between devices, per_device(): lax.all_gather(inputs, 'tensor', axis=1, tiled=True).astype(jnp.float32)  32.9 us
    reduce_scatter x1, waiting for transfers between devices, per_device(): lax.psum_scatter(contract_cols(pre_grad, proj_weight).astype(jnp.bfloat16...  31.7 us
    all_to_all x1, waiting for transfers between devices, per_device(): lax.all_to_all(input_grad, 'tensor', split_axis=1, concat_axis=0, tiled=T...  10.7 us
    dot_general x1, matrix products, contract_cols(): lax.dot_general(left, right, (((1,), (1,)), ((), ())), preferred_element_...  7.06 us
    mul x1, other arithmetic, per_device(): unit_rows = centred * inv_std  5.68 us
    all_to_all x1, starting transfers between devices, per_device(): lax.all_to_all(send_slots, 'dp', split_axis=0, concat_axis=0, tiled=True)  5.52 us
    all_to_all x1, starting transfers between devices, per_device(): lax.all_to_all(send_rows, 'dp', split_axis=0, concat_axis=0, tiled=True)  4.29 us
  transfers between devices with their start and end apart: 5, of which 5 were waited for; matrix products, arithmetic and copies ran while one was open for 6% of the time, Pallas kernels for 0%

commit v1 on v0

v1 whole, which is shorter than its diff:
```python
import functools
import math

import jax
import jax.numpy as jnp
from jax import lax
from jax.experimental import pallas as pl
from jax.experimental.pallas import tpu as pltpu
from jax.sharding import PartitionSpec as P

epsilon = 1e-05
MESH = pl.DeviceIdType.MESH
f32, bf16 = jnp.float32, jnp.bfloat16
LANES = 128


def rows_by_cols(left, right):
    return lax.dot_general(
        left, right, (((1,), (1,)), ((), ())), preferred_element_type=f32
    )


def kernel(
    n_dp, n_t, cap,
    x_ref, up_ref, w_ref, bias_ref, gain_ref, hr_col_ref, hr_row_ref,
    out_ref,
    weights, packed, arrived, slots_out, slots_in, home, centred,
    part_out, part_in, stat_out, stat_in, grads, sums,
    w_send, w_recv, row_send, row_recv, slot_send, slot_recv,
    part_send, part_recv, stat_send, stat_recv, grad_send, grad_recv, sum_send, sum_recv,
    local_sem,
):
    me = lax.axis_index("dp")
    t = lax.axis_index("tensor")
    rows, cols = x_ref.shape
    head = up_ref.shape[1]
    width = cols + head
    depth = n_t * cols
    per = LANES // cap

    def sibling(u):
        return u + 1 - 2 * lax.rem(u, 2)

    peers = []
    for k in range(1, n_t // 2):
        u = lax.rem(t + 2 * k, n_t)
        peers += [u, sibling(u)]
    peers.append(sibling(t))
    dests = [lax.rem(me + d, n_dp) for d in range(1, n_dp)]
    sources = [lax.rem(me + n_dp - d, n_dp) for d in range(1, n_dp)]

    barrier = pltpu.get_barrier_semaphore()
    for u in peers:
        pl.semaphore_signal(barrier, inc=1, device_id={"tensor": u}, device_id_type=MESH)
    for j in dests:
        pl.semaphore_signal(barrier, inc=1, device_id={"dp": j}, device_id_type=MESH)

    own_w = pltpu.make_async_copy(
        w_ref.at[pl.ds(pl.multiple_of(t * cols, LANES), cols)], weights.at[t], local_sem.at[0]
    )
    own_w.start()

    hr_col, hr_row = hr_col_ref[...], hr_row_ref[...]
    owner_col, owner_row = hr_col // rows, hr_row // rows
    slot_col = hr_col - owner_col * rows
    down = lax.broadcasted_iota(jnp.int32, (rows, rows), 0)
    across = lax.broadcasted_iota(jnp.int32, (rows, rows), 1)
    same = owner_col == owner_row
    rank_row = jnp.sum(jnp.where(same & (down < across), 1.0, 0.0), axis=0, keepdims=True).astype(jnp.int32)
    rank_col = jnp.sum(jnp.where(same & (across < down), 1.0, 0.0), axis=1, keepdims=True).astype(jnp.int32)
    target_row = owner_row * cap + rank_row
    total_slots = n_dp * cap
    placing = jnp.where(
        lax.broadcasted_iota(jnp.int32, (total_slots, rows), 0) == target_row, 1.0, 0.0
    ).astype(bf16)
    chunk = math.gcd(cols, 256)
    for c in range(0, cols, chunk):
        packed[:, c : c + chunk] = jnp.dot(
            placing, x_ref[:, c : c + chunk], preferred_element_type=f32
        ).astype(bf16)
    packed[:, cols:] = jnp.dot(placing, up_ref[...], preferred_element_type=f32).astype(bf16)
    lane = lax.broadcasted_iota(jnp.int32, (rows, LANES), 1)
    my_lane = lax.rem(me, per) * cap
    for j in range(n_dp):
        hit = (owner_col == j) & (rank_col + my_lane == lane)
        line = jnp.sum(jnp.where(hit, slot_col.astype(f32) + 1.0, 0.0), axis=0, keepdims=True)
        slots_out[j] = jnp.broadcast_to(line, (8, LANES)).astype(jnp.int32)

    def w_copy(u, src_slot):
        return pltpu.make_async_remote_copy(
            src_ref=w_ref.at[pl.ds(pl.multiple_of(u * cols, LANES), cols)],
            dst_ref=weights.at[src_slot],
            send_sem=w_send.at[u], recv_sem=w_recv.at[src_slot],
            device_id={"tensor": u}, device_id_type=MESH,
        )

    def row_copy(j, src_slot):
        return pltpu.make_async_remote_copy(
            src_ref=packed.at[pl.ds(pl.multiple_of(j * cap, 16), cap)],
            dst_ref=arrived.at[pl.ds(pl.multiple_of(src_slot * cap, 16), cap)],
            send_sem=row_send.at[j], recv_sem=row_recv.at[src_slot],
            device_id={"dp": j}, device_id_type=MESH,
        )

    def slot_copy(j, src_slot):
        return pltpu.make_async_remote_copy(
            src_ref=slots_out.at[j], dst_ref=slots_in.at[src_slot],
            send_sem=slot_send.at[j], recv_sem=slot_recv.at[src_slot],
            device_id={"dp": j}, device_id_type=MESH,
        )

    def tensor_copy(src, dst, send, recv, u, src_slot):
        return pltpu.make_async_remote_copy(
            src_ref=src, dst_ref=dst.at[src_slot],
            send_sem=send.at[u], recv_sem=recv.at[src_slot],
            device_id={"tensor": u}, device_id_type=MESH,
        )

    pl.semaphore_wait(barrier, len(peers) + len(dests))
    for u in peers:
        w_copy(u, t).start()
    for j in dests:
        slot_copy(j, me).start()
        row_copy(j, me).start()
    own_rows = pltpu.make_async_copy(
        packed.at[pl.ds(pl.multiple_of(me * cap, 16), cap)],
        arrived.at[pl.ds(pl.multiple_of(me * cap, 16), cap)],
        local_sem.at[1],
    )
    own_rows.start()
    slots_in[me] = slots_out[me]

    gain = gain_ref[pl.ds(t, 1), :]
    gain_hi = gain.astype(bf16)
    gain_rest = gain - gain_hi.astype(f32)
    gain_mid = gain_rest.astype(bf16)
    gain_lo = (gain_rest - gain_mid.astype(f32)).astype(bf16)
    which = lax.broadcasted_iota(jnp.int32, (16, cols), 0)
    gain_parts = jnp.where(
        which == 0, gain_hi.astype(f32),
        jnp.where(which == 1, gain_mid.astype(f32), jnp.where(which == 2, gain_lo.astype(f32), 0.0)),
    ).astype(bf16)

    def weighted_sum(u):
        stat_out[u] = jnp.zeros(stat_out.shape[1:], f32)
        line = jnp.sum(jnp.dot(gain_parts, weights[u], preferred_element_type=f32), axis=0, keepdims=True)
        stat_out[u, 2:3, :] = line

    own_w.wait()
    weighted_sum(t)
    for u in reversed(peers):
        w_copy(u, u).wait_recv()
        weighted_sum(u)

    for i in sources:
        slot_copy(i, i).wait_recv()
    lines = []
    for g in range(n_dp // per):
        line = slots_in[g * per, 0:1, :]
        for k in range(1, per):
            line = line + slots_in[g * per + k, 0:1, :]
        lines.append(line)
    slot_line = jnp.concatenate(lines, axis=1) - 1
    landing = jnp.where(
        lax.broadcasted_iota(jnp.int32, (rows, total_slots), 0) == slot_line, 1.0, 0.0
    ).astype(bf16)
    own_rows.wait()
    for i in sources:
        row_copy(i, i).wait_recv()
    running = jnp.zeros((rows, LANES), f32)
    for c in range(0, cols, chunk):
        piece = jnp.dot(landing, arrived[:, c : c + chunk], preferred_element_type=f32)
        home[:, c : c + chunk] = piece.astype(bf16)
        for q in range(0, chunk, LANES):
            running = running + piece[:, q : q + LANES]
    home[:, cols:] = jnp.dot(landing, arrived[:, cols:], preferred_element_type=f32).astype(bf16)
    mean_here = jnp.sum(running, axis=1, keepdims=True) / cols
    running = jnp.zeros((rows, LANES), f32)
    for c in range(0, cols, chunk):
        piece = home[:, c : c + chunk].astype(f32) - mean_here
        centred[:, c : c + chunk] = (piece * gain[:, c : c + chunk]).astype(bf16)
        square = piece * piece
        for q in range(0, chunk, LANES):
            running = running + square[:, q : q + LANES]
    moment_here = jnp.sum(running, axis=1, keepdims=True)

    eye = down == across

    def to_row(column):
        return jnp.sum(jnp.where(eye, column, 0.0), axis=0, keepdims=True)

    def to_col(line):
        return jnp.sum(jnp.where(eye, line, 0.0), axis=1, keepdims=True)

    mean_line, moment_line = to_row(mean_here), to_row(moment_here)
    for u in peers + [t]:
        stat_out[u, 0:1, :] = mean_line
        stat_out[u, 1:2, :] = moment_line
    for u in peers:
        tensor_copy(stat_out.at[u], stat_in, stat_send, stat_recv, u, t).start()
    for u in peers:
        part_out[u] = jnp.dot(centred[...], weights[u], preferred_element_type=f32).astype(bf16)
        tensor_copy(part_out.at[u], part_in, part_send, part_recv, u, t).start()
    total = jnp.dot(centred[...], weights[t], preferred_element_type=f32)

    stat_in[t] = stat_out[t]
    for u in peers:
        tensor_copy(stat_out.at[u], stat_in, stat_send, stat_recv, u, u).wait_recv()
    mean_all = stat_in[0, 0:1, :]
    moment_all = stat_in[0, 1:2, :]
    weighted = stat_in[0, 2:3, :]
    for u in range(1, n_t):
        mean_all = mean_all + stat_in[u, 0:1, :]
        moment_all = moment_all + stat_in[u, 1:2, :]
        weighted = weighted + stat_in[u, 2:3, :]
    mean_all = mean_all / n_t
    for u in range(n_t):
        away = stat_in[u, 0:1, :] - mean_all
        moment_all = moment_all + cols * away * away
        total = total + to_col(away) * stat_in[u, 2:3, :]
    scale = to_col(lax.rsqrt(moment_all / depth + epsilon))
    mean_col = to_col(mean_all)
    for u in peers:
        tensor_copy(part_out.at[u], part_in, part_send, part_recv, u, u).wait_recv()
        total = total + part_in[u].astype(f32)
    product = scale * total
    preact = product + bias_ref[...]
    gate = 1.0 / (1.0 + jnp.exp(-preact))
    grad = (home[:, cols:].astype(f32) * gate * (1.0 + preact * (1.0 - gate))).astype(bf16)
    grads[t] = grad
    for u in peers:
        tensor_copy(grads.at[t], grads, grad_send, grad_recv, u, t).start()
    wide = grad.astype(f32)
    sums[t] = jnp.zeros(sums.shape[1:], f32)
    sums[t, 0:1, :] = to_row(jnp.sum(wide * weighted, axis=1, keepdims=True))
    sums[t, 1:2, :] = to_row(jnp.sum(wide * product, axis=1, keepdims=True))
    for u in peers:
        tensor_copy(sums.at[t], sums, sum_send, sum_recv, u, t).start()
    for u in peers:
        tensor_copy(sums.at[t], sums, sum_send, sum_recv, u, u).wait_recv()
    both = sums[0]
    for u in range(1, n_t):
        both = both + sums[u]
    mean_grad = to_col(both[0:1, :]) / depth
    mean_unit = to_col(both[1:2, :]) / depth * scale
    for u in peers:
        tensor_copy(grads.at[t], grads, grad_send, grad_recv, u, u).wait_recv()
    for c in range(0, cols, chunk):
        piece = rows_by_cols(grads[0], weights[0, c : c + chunk, :])
        for u in range(1, n_t):
            piece = piece + rows_by_cols(grads[u], weights[u, c : c + chunk, :])
        piece = piece * gain[:, c : c + chunk]
        away = home[:, c : c + chunk].astype(f32) - mean_col
        out_ref[:, c : c + chunk] = (scale * (piece - mean_grad - away * mean_unit)).astype(bf16)

    for u in peers:
        w_copy(u, t).wait_send()
        tensor_copy(stat_out.at[u], stat_in, stat_send, stat_recv, u, t).wait_send()
        tensor_copy(part_out.at[u], part_in, part_send, part_recv, u, t).wait_send()
        tensor_copy(grads.at[t], grads, grad_send, grad_recv, u, t).wait_send()
        tensor_copy(sums.at[t], sums, sum_send, sum_recv, u, t).wait_send()
    for j in dests:
        slot_copy(j, me).wait_send()
        row_copy(j, me).wait_send()


def per_device(inputs, upstream, proj_weight, proj_bias, norm_gain, home_rows):
    n_dp, n_t = lax.axis_size("dp"), lax.axis_size("tensor")
    rows, cols = inputs.shape
    head = upstream.shape[1]
    cap = max(2, 2 * rows // n_dp)
    width = cols + head
    line = max(rows, head)
    dma = pltpu.SemaphoreType.DMA
    in_vmem = pl.BlockSpec(memory_space=pltpu.VMEM)
    return pl.pallas_call(
        functools.partial(kernel, n_dp, n_t, cap),
        out_shape=jax.ShapeDtypeStruct((rows, cols), bf16),
        in_specs=[in_vmem, in_vmem, pl.BlockSpec(memory_space=pl.ANY)] + [in_vmem] * 4,
        out_specs=in_vmem,
        scratch_shapes=[
            pltpu.VMEM((n_t, cols, head), bf16),
            pltpu.VMEM((n_dp * cap, width), bf16),
            pltpu.VMEM((n_dp * cap, width), bf16),
            pltpu.VMEM((n_dp, 8, LANES), jnp.int32),
            pltpu.VMEM((n_dp, 8, LANES), jnp.int32),
            pltpu.VMEM((rows, width), bf16),
            pltpu.VMEM((rows, cols), bf16),
            pltpu.VMEM((n_t, rows, head), bf16),
            pltpu.VMEM((n_t, rows, head), bf16),
            pltpu.VMEM((n_t, 8, line), f32),
            pltpu.VMEM((n_t, 8, line), f32),
            pltpu.VMEM((n_t, rows, head), bf16),
            pltpu.VMEM((n_t, 8, line), f32),
        ]
        + [dma((n_t,))] * 2
        + [dma((n_dp,))] * 4
        + [dma((n_t,))] * 8
        + [dma((2,))],
        compiler_params=pltpu.CompilerParams(
            collective_id=0, has_side_effects=True, vmem_limit_bytes=48 * 1024 * 1024
        ),
        cost_estimate=pl.CostEstimate(
            flops=8 * rows * cols * head * n_t, bytes_accessed=2 * n_t * cols * head, transcendentals=rows * head
        ),
    )(
        inputs,
        upstream,
        proj_weight,
        proj_bias.reshape(1, head),
        norm_gain.reshape(n_t, cols),
        home_rows.reshape(rows, 1),
        home_rows.reshape(1, rows),
    )


def solution(mesh):
    return jax.shard_map(
        per_device,
        mesh=mesh,
        in_specs=(
            P("dp", "tensor"),
            P("dp", "tensor"),
            P(None, "tensor"),
            P("tensor"),
            P(),
            P("dp"),
        ),
        out_specs=P("dp", "tensor"),
        check_vma=False,
    )
```

time: 172 us -> 71.8 us (0.42)
  the two profiles are of different devices: /device:TPU:0 before, /device:TPU:15 now
where the time goes in v1:
time: 71.8 us; the launch traced here: 71.5 us
  Pallas kernels  63.7 us (89%)
  local copies, waits for them, and re-layouts  7.72 us (11%)
    pallas_call x1, Pallas kernels, per_device(): pl.pallas_call(functools.partial(kernel, n_dp, n_t, cap), out_shape=jax.S...  63.7 us
    unnamed x11, local copies, waits for them, and re-layouts  6.16 us

profile of v1, /device:TPU:15, one launch (start us, length us, event | category | flops | bytes accessed | tf_op | source)
XLA Modules:
  0.0 71.5 jit_solution(17387143353730238096)
XLA Ops:
  0.0 0.8 %reshape.13.gain_ref = f32[4,1536]{1,0:T(4,128)S(1)} reshape(f32[6144]{0:T(1024)} %param.10) | data formatting | bytes 49152 | tf_op jit(solution)/shard_map/reshape | solution.py:311
  0.8 0.8 %copy.7.hr_col_ref = s32[256,1]{1,0:T(8,128)S(1)} copy(s32[256,1]{0,1:T(1,128)} %bitcast.3) | data formatting | bytes 2048 | tf_op jit(solution)/shard_map/reshape | solution.py:312
  1.6 0.0 copy-start
  1.6 0.7 copy-done
  2.3 0.0 copy-start.1
  2.3 1.9 %copy-done.1 = bf16[6144,256]{1,0:T(8,128)(2,1)S(1)} copy-done((bf16[6144,256]{1,0:T(8,128)(2,1)S(1)}, bf16[6144,256]{1,0:T(8,128)(2,1)}, u32[]{:S(2)}) %copy-start.1) | copy-done | bytes 3145752
  4.1 0.0 copy-start.2
  4.1 1.1 %copy-done.2 = bf16[256,1536]{1,0:T(8,128)(2,1)S(1)} copy-done((bf16[256,1536]{1,0:T(8,128)(2,1)S(1)}, bf16[256,1536]{1,0:T(8,128)(2,1)}, u32[]{:S(2)}) %copy-start.2) | copy-done | bytes 786456
  5.3 0.0 copy-start.3
  5.3 0.9 %copy-done.3 = bf16[256,256]{1,0:T(8,128)(2,1)S(1)} copy-done((bf16[256,256]{1,0:T(8,128)(2,1)S(1)}, bf16[256,256]{1,0:T(8,128)(2,1)}, u32[]{:S(2)}) %copy-start.3) | copy-done | bytes 131096
  6.2 0.0 copy-start.4
  6.2 0.7 copy-done.4
  6.9 63.7 %shard_map.64 = bf16[256,1536]{1,0:T(8,128)(2,1)S(1)} custom-call(bf16[256,1536]{1,0:T(8,128)(2,1)S(1)} %copy-done.2, bf16[256,256]{1,0:T(8,128)(2,1)S(1)} %copy-done.3, bf16[6144,256]{1,0:T(8,128)(2,1)S(1)} %copy-done.1, f32[1,256]{1,0:T(1,128)S(1)} %bitcast.5, f32[4,1536]{1,0:T(4,128)S(1)} %reshape.13.gain_ref, s32[256,1]{1,0:T(8,128)S(1)} %copy.7.hr_col_ref, ...), custom_call_target="tpu_custom_call" | custom-call | flops 3221225472 | bytes 3145728 | tf_op jit(solution)/shard_map/pallas_call | solution.py:276
  70.6 0.9 %copy.9 = bf16[256,1536]{1,0:T(8,128)(2,1)} copy(bf16[256,1536]{1,0:T(8,128)(2,1)S(1)} %shard_map.64) | data formatting | bytes 1572864
Async XLA Ops:
  1.6 0.7 copy-start
  2.3 1.9 %copy-start.1 = (bf16[6144,256]{1,0:T(8,128)(2,1)S(1)}, bf16[6144,256]{1,0:T(8,128)(2,1)}, u32[]{:S(2)}) copy-start(bf16[6144,256]{1,0:T(8,128)(2,1)} %w_ref.1) | copy-start | bytes 9437188
  4.1 1.1 %copy-start.2 = (bf16[256,1536]{1,0:T(8,128)(2,1)S(1)}, bf16[256,1536]{1,0:T(8,128)(2,1)}, u32[]{:S(2)}) copy-start(bf16[256,1536]{1,0:T(8,128)(2,1)} %x_ref.1) | copy-start | bytes 2359300
  5.3 0.9 %copy-start.3 = (bf16[256,256]{1,0:T(8,128)(2,1)S(1)}, bf16[256,256]{1,0:T(8,128)(2,1)}, u32[]{:S(2)}) copy-start(bf16[256,256]{1,0:T(8,128)(2,1)} %up_ref.1) | copy-start | bytes 393220
  6.2 0.7 copy-start.4

commit v2 on v1

--- a/solution.py
+++ b/solution.py
@@ -22,8 +22,9 @@
 
 def kernel(
     n_dp, n_t, cap,
-    x_ref, up_ref, w_ref, bias_ref, gain_ref, hr_col_ref, hr_row_ref,
+    x_hbm, up_hbm, w_ref, bias_hbm, gain_hbm, hr_hbm,
     out_ref,
+    x_ref, up_ref, bias_ref, gain_ref, hr_ref,
     weights, packed, arrived, slots_out, slots_in, home, centred,
     part_out, part_in, stat_out, stat_in, grads, sums,
     w_send, w_recv, row_send, row_recv, slot_send, slot_recv,
@@ -58,13 +59,30 @@
     own_w = pltpu.make_async_copy(
         w_ref.at[pl.ds(pl.multiple_of(t * cols, LANES), cols)], weights.at[t], local_sem.at[0]
     )
+    fetches = [
+        pltpu.make_async_copy(src, dst, local_sem.at[2 + k])
+        for k, (src, dst) in enumerate(
+            [
+                (hr_hbm, hr_ref),
+                (x_hbm, x_ref),
+                (up_hbm, up_ref),
+                (gain_hbm.at[:, pl.ds(pl.multiple_of(t * cols, LANES), cols)], gain_ref),
+                (bias_hbm, bias_ref),
+            ]
+        )
+    ]
+    for fetch in fetches:
+        fetch.start()
     own_w.start()
 
-    hr_col, hr_row = hr_col_ref[...], hr_row_ref[...]
+    fetches[0].wait()
+    hr_row = hr_ref[...]
+    down = lax.broadcasted_iota(jnp.int32, (rows, rows), 0)
+    across = lax.broadcasted_iota(jnp.int32, (rows, rows), 1)
+    eye = down == across
+    hr_col = jnp.sum(jnp.where(eye, hr_row.astype(f32), 0.0), axis=1, keepdims=True).astype(jnp.int32)
     owner_col, owner_row = hr_col // rows, hr_row // rows
     slot_col = hr_col - owner_col * rows
-    down = lax.broadcasted_iota(jnp.int32, (rows, rows), 0)
-    across = lax.broadcasted_iota(jnp.int32, (rows, rows), 1)
     same = owner_col == owner_row
     rank_row = jnp.sum(jnp.where(same & (down < across), 1.0, 0.0), axis=0, keepdims=True).astype(jnp.int32)
     rank_col = jnp.sum(jnp.where(same & (across < down), 1.0, 0.0), axis=1, keepdims=True).astype(jnp.int32)
@@ -74,6 +92,8 @@
         lax.broadcasted_iota(jnp.int32, (total_slots, rows), 0) == target_row, 1.0, 0.0
     ).astype(bf16)
     chunk = math.gcd(cols, 256)
+    fetches[1].wait()
+    fetches[2].wait()
     for c in range(0, cols, chunk):
         packed[:, c : c + chunk] = jnp.dot(
             placing, x_ref[:, c : c + chunk], preferred_element_type=f32
@@ -130,7 +150,9 @@
     own_rows.start()
     slots_in[me] = slots_out[me]
 
-    gain = gain_ref[pl.ds(t, 1), :]
+    fetches[3].wait()
+    fetches[4].wait()
+    gain = gain_ref[...]
     gain_hi = gain.astype(bf16)
     gain_rest = gain - gain_hi.astype(f32)
     gain_mid = gain_rest.astype(bf16)
@@ -184,8 +206,6 @@
             running = running + square[:, q : q + LANES]
     moment_here = jnp.sum(running, axis=1, keepdims=True)
 
-    eye = down == across
-
     def to_row(column):
         return jnp.sum(jnp.where(eye, column, 0.0), axis=0, keepdims=True)
 
@@ -276,9 +296,14 @@
     return pl.pallas_call(
         functools.partial(kernel, n_dp, n_t, cap),
         out_shape=jax.ShapeDtypeStruct((rows, cols), bf16),
-        in_specs=[in_vmem, in_vmem, pl.BlockSpec(memory_space=pl.ANY)] + [in_vmem] * 4,
+        in_specs=[pl.BlockSpec(memory_space=pltpu.HBM)] * 6,
         out_specs=in_vmem,
         scratch_shapes=[
+            pltpu.VMEM((rows, cols), bf16),
+            pltpu.VMEM((rows, head), bf16),
+            pltpu.VMEM((1, head), f32),
+            pltpu.VMEM((1, cols), f32),
+            pltpu.VMEM((1, rows), jnp.int32),
             pltpu.VMEM((n_t, cols, head), bf16),
             pltpu.VMEM((n_dp * cap, width), bf16),
             pltpu.VMEM((n_dp * cap, width), bf16),
@@ -296,9 +321,9 @@
         + [dma((n_t,))] * 2
         + [dma((n_dp,))] * 4
         + [dma((n_t,))] * 8
-        + [dma((2,))],
+        + [dma((7,))],
         compiler_params=pltpu.CompilerParams(
-            collective_id=0, has_side_effects=True, vmem_limit_bytes=48 * 1024 * 1024
+            collective_id=0, has_side_effects=True, vmem_limit_bytes=64 * 1024 * 1024
         ),
         cost_estimate=pl.CostEstimate(
             flops=8 * rows * cols * head * n_t, bytes_accessed=2 * n_t * cols * head, transcendentals=rows * head
@@ -308,8 +333,7 @@
         upstream,
         proj_weight,
         proj_bias.reshape(1, head),
-        norm_gain.reshape(n_t, cols),
-        home_rows.reshape(rows, 1),
+        norm_gain.reshape(1, n_t * cols),
         home_rows.reshape(1, rows),
     )
 

time: 71.8 us -> 65.6 us (0.914)
  the two profiles are of different devices: /device:TPU:15 before, /device:TPU:13 now
where the time goes in v2:
time: 65.6 us; the launch traced here: 65.5 us
  Pallas kernels  63.4 us (97%)
  local copies, waits for them, and re-layouts  2.06 us (3%)
    pallas_call x1, Pallas kernels, per_device(): pl.pallas_call(functools.partial(kernel, n_dp, n_t, cap), out_shape=jax.S...  63.4 us
    unnamed x1, local copies, waits for them, and re-layouts  2.06 us

profile of v2, /device:TPU:13, one launch (start us, length us, event | category | flops | bytes accessed | tf_op | source)
XLA Modules:
  0.0 65.5 jit_solution(11236315377158149824)
XLA Ops:
  0.0 63.4 %shard_map.64 = bf16[256,1536]{1,0:T(8,128)(2,1)} custom-call(bf16[256,1536]{1,0:T(8,128)(2,1)} %x_hbm.1, bf16[256,256]{1,0:T(8,128)(2,1)} %up_hbm.1, bf16[6144,256]{1,0:T(8,128)(2,1)} %w_ref.1, f32[1,256]{1,0:T(1,128)} %bitcast.4, f32[1,6144]{1,0:T(1,128)} %bitcast.3, s32[1,256]{1,0:T(1,128)} %bitcast.5), custom_call_target="tpu_custom_call" | custom-call | flops 3221225472 | bytes 3145728 | tf_op jit(solution)/shard_map/pallas_call | solution.py:296
  63.4 2.1 %copy.8 = bf16[256,1536]{1,0:T(8,128)(2,1)} copy(bf16[256,1536]{1,0:T(8,128)(2,1)} %shard_map.64) | data formatting | bytes 1572864

commit v3 on v2

v3 whole, which is shorter than its diff:
```python
import functools
import math

import jax
import jax.numpy as jnp
from jax import lax
from jax.experimental import pallas as pl
from jax.experimental.pallas import tpu as pltpu
from jax.sharding import PartitionSpec as P

epsilon = 1e-05
MESH = pl.DeviceIdType.MESH
f32, bf16 = jnp.float32, jnp.bfloat16
LANES = 128


def rows_by_cols(left, right):
    return lax.dot_general(
        left, right, (((1,), (1,)), ((), ())), preferred_element_type=f32
    )


def kernel(
    n_dp, n_t, cap,
    x_hbm, up_hbm, w_ref, bias_hbm, gain_hbm, hr_hbm,
    out_ref,
    blocks, up_ref, bias_ref, gain_ref, hr_ref, w_head,
    weights, packed, arrived, slots_out, slots_in, facts_out, facts_in,
    centred, grads_out, grads_in, grads, sums,
    x_send, x_recv, x_pass, w_send, w_recv, w_pass, w_got, near_send, near_recv,
    row_send, row_recv, slot_send, slot_recv, fact_send, fact_recv, back_send, back_recv,
    grad_send, grad_recv, sum_send, sum_recv,
    local_sem,
):
    me = lax.axis_index("dp")
    t = lax.axis_index("tensor")
    rows, head = up_ref.shape
    cols = blocks.shape[2]
    depth = n_t * cols
    per = LANES // cap
    chunk = math.gcd(cols, 256)
    first = 2 * cols // 3 // LANES * LANES
    parts = [(0, first), (first, cols - first)]
    quarter = cols // 4

    def sibling(u):
        return u + 1 - 2 * lax.rem(u, 2)

    across_peers = [lax.rem(t + 2 * k, n_t) for k in range(1, n_t // 2)]
    other_peers = [sibling(u) for u in across_peers]
    far = [u for pair in zip(across_peers, other_peers) for u in pair]
    near = sibling(t)
    peers = far + [near]
    partner = sibling(me)
    half = lax.rem(me, 2)
    dests = [lax.rem(me + d, n_dp) for d in range(1, n_dp)]
    sources = [lax.rem(me + n_dp - d, n_dp) for d in range(1, n_dp)]

    barrier = pltpu.get_barrier_semaphore()
    for u in peers:
        pl.semaphore_signal(barrier, inc=1, device_id={"tensor": u}, device_id_type=MESH)
    for j in dests:
        pl.semaphore_signal(barrier, inc=1, device_id={"dp": j}, device_id_type=MESH)

    fetches = [
        pltpu.make_async_copy(src, dst, local_sem.at[k])
        for k, (src, dst) in enumerate(
            [
                (hr_hbm, hr_ref),
                (x_hbm, blocks.at[t]),
                (up_hbm, up_ref),
                (gain_hbm, gain_ref),
                (bias_hbm, bias_ref),
                (w_ref, w_head),
                (w_ref.at[pl.ds(pl.multiple_of(t * cols, LANES), cols)], weights.at[t]),
            ]
        )
    ]
    for fetch in fetches:
        fetch.start()

    fetches[0].wait()
    hr_row = hr_ref[...]
    down = lax.broadcasted_iota(jnp.int32, (rows, rows), 0)
    across = lax.broadcasted_iota(jnp.int32, (rows, rows), 1)
    eye = down == across

    def to_row(column):
        return jnp.sum(jnp.where(eye, column, 0.0), axis=0, keepdims=True)

    def to_col(line):
        return jnp.sum(jnp.where(eye, line, 0.0), axis=1, keepdims=True)

    hr_col = to_col(hr_row.astype(f32)).astype(jnp.int32)
    owner_col, owner_row = hr_col // rows, hr_row // rows
    slot_col = hr_col - owner_col * rows
    same = owner_col == owner_row
    rank_row = jnp.sum(jnp.where(same & (down < across), 1.0, 0.0), axis=0, keepdims=True).astype(jnp.int32)
    rank_col = jnp.sum(jnp.where(same & (across < down), 1.0, 0.0), axis=1, keepdims=True).astype(jnp.int32)
    target_row = owner_row * cap + rank_row
    total_slots = n_dp * cap
    placing = jnp.where(
        lax.broadcasted_iota(jnp.int32, (total_slots, rows), 0) == target_row, 1.0, 0.0
    ).astype(bf16)
    fetches[1].wait()
    for c in range(0, cols, chunk):
        packed[:, c : c + chunk] = jnp.dot(
            placing, blocks[t, :, c : c + chunk], preferred_element_type=f32
        ).astype(bf16)
    lane = lax.broadcasted_iota(jnp.int32, (rows, LANES), 1)
    my_lane = lax.rem(me, per) * cap

    def in_lanes(j, column):
        hit = (owner_col == j) & (rank_col + my_lane == lane)
        return jnp.sum(jnp.where(hit, column, 0.0), axis=0, keepdims=True)

    for j in range(n_dp):
        slots_out[j] = jnp.broadcast_to(in_lanes(j, slot_col.astype(f32) + 1.0), (8, LANES)).astype(jnp.int32)

    def remote(src, dst, send, recv, to):
        return pltpu.make_async_remote_copy(
            src_ref=src, dst_ref=dst, send_sem=send, recv_sem=recv, device_id=to, device_id_type=MESH
        )

    def x_copy(u, block):
        return remote(blocks.at[block], blocks.at[block], x_send.at[u], x_recv.at[block], {"tensor": u})

    def x_forward(block):
        return remote(blocks.at[block], blocks.at[block], x_pass.at[block], x_recv.at[block], {"tensor": near})

    def near_copy(block):
        return remote(
            w_ref.at[pl.ds(pl.multiple_of(near * cols, LANES), cols)], weights.at[block],
            near_send.at[0], near_recv.at[0], {"tensor": near},
        )

    def w_span(which, q):
        return pl.ds(pl.multiple_of((2 * which + q) * quarter, 16), quarter)

    def w_copy(u, block, q):
        start = pl.multiple_of(u * cols + (2 * half + q) * quarter, 16)
        return remote(
            w_ref.at[pl.ds(start, quarter)], weights.at[block, w_span(half, q)],
            w_send.at[u, q], w_recv.at[block, q], {"tensor": u},
        )

    def w_forward(block, q, which):
        return remote(
            weights.at[block, w_span(which, q)], weights.at[block, w_span(which, q)],
            w_pass.at[block, q], w_got.at[block, q], {"dp": partner},
        )

    def row_copy(j, source, k):
        begin, size = parts[k]
        return remote(
            packed.at[pl.ds(pl.multiple_of(j * cap, 16), cap), pl.ds(begin, size)],
            arrived.at[pl.ds(pl.multiple_of(source * cap, 16), cap), pl.ds(begin, size)],
            row_send.at[k, j], row_recv.at[k, source], {"dp": j},
        )

    def back_copy(j, source):
        return remote(
            grads_out.at[pl.ds(pl.multiple_of(j * cap, 16), cap)],
            grads_in.at[pl.ds(pl.multiple_of(source * cap, 16), cap)],
            back_send.at[j], back_recv.at[source], {"dp": j},
        )

    def slot_copy(j, source):
        return remote(slots_out.at[j], slots_in.at[source], slot_send.at[j], slot_recv.at[source], {"dp": j})

    def fact_copy(j, source):
        return remote(facts_out.at[j], facts_in.at[source], fact_send.at[j], fact_recv.at[source], {"dp": j})

    def grad_copy(u, block):
        return remote(grads.at[block], grads.at[block], grad_send.at[u], grad_recv.at[block], {"tensor": u})

    def sum_copy(u, block):
        return remote(sums.at[block], sums.at[block], sum_send.at[u], sum_recv.at[block], {"tensor": u})

    pl.semaphore_wait(barrier, len(peers) + len(dests))
    for u in across_peers:
        x_copy(u, t).start()
    x_copy(near, t).start()
    for j in dests:
        slot_copy(j, me).start()
        row_copy(j, me, 0).start()
    near_copy(t).start()
    own_rows = pltpu.make_async_copy(
        packed.at[pl.ds(pl.multiple_of(me * cap, 16), cap)],
        arrived.at[pl.ds(pl.multiple_of(me * cap, 16), cap)],
        local_sem.at[7],
    )
    own_rows.start()
    slots_in[me] = slots_out[me]

    for fetch in fetches[2:]:
        fetch.wait()
    weighted = jnp.zeros((1, head), f32)
    which = lax.broadcasted_iota(jnp.int32, (16, cols), 0)
    for b in range(n_t):
        gain = gain_ref[:, b * cols : (b + 1) * cols]
        gain_hi = gain.astype(bf16).astype(f32)
        gain_mid = (gain - gain_hi).astype(bf16).astype(f32)
        gain_lo = gain - gain_hi - gain_mid
        gain_parts = jnp.where(
            which == 0, gain_hi, jnp.where(which == 1, gain_mid, jnp.where(which == 2, gain_lo, 0.0))
        ).astype(bf16)
        line = jnp.dot(gain_parts, w_head[b * cols : (b + 1) * cols, :], preferred_element_type=f32)
        weighted = weighted + jnp.sum(line, axis=0, keepdims=True)

    for u in across_peers:
        x_copy(u, u).wait_recv()
        x_forward(u).start()
    for q in range(2):
        for u in far:
            w_copy(u, t, q).start()
    x_copy(near, near).wait_recv()
    for u in other_peers:
        x_forward(u).wait_recv()
    running = jnp.zeros((rows, LANES), f32)
    for b in range(n_t):
        for c in range(0, cols, LANES):
            running = running + blocks[b, :, c : c + LANES].astype(f32)
    mean_here = jnp.sum(running, axis=1, keepdims=True) / depth
    running = jnp.zeros((rows, LANES), f32)
    total = jnp.zeros((rows, head), f32)
    for b in range(n_t):
        for c in range(0, cols, LANES):
            piece = blocks[b, :, c : c + LANES].astype(f32) - mean_here
            gain = gain_ref[:, b * cols + c : b * cols + c + LANES]
            centred[:, c : c + LANES] = (piece * gain).astype(bf16)
            running = running + piece * piece
        total = total + jnp.dot(
            centred[...], w_head[b * cols : (b + 1) * cols, :], preferred_element_type=f32
        )
    scale_here = lax.rsqrt(jnp.sum(running, axis=1, keepdims=True) / depth + epsilon)
    product = scale_here * total
    preact = product + bias_ref[...]
    gate = 1.0 / (1.0 + jnp.exp(-preact))
    grad = (up_ref[...].astype(f32) * gate * (1.0 + preact * (1.0 - gate))).astype(bf16)
    grads_out[...] = jnp.dot(placing, grad, preferred_element_type=f32).astype(bf16)
    wide = grad.astype(f32)
    facts = [
        mean_here,
        scale_here,
        jnp.sum(wide * weighted, axis=1, keepdims=True),
        jnp.sum(wide * product, axis=1, keepdims=True),
    ]
    for j in range(n_dp):
        facts_out[j] = jnp.zeros((8, LANES), f32)
        for k, fact in enumerate(facts):
            facts_out[j, k : k + 1, :] = in_lanes(j, fact)
    for j in dests:
        back_copy(j, me).start()
        fact_copy(j, me).start()
    for j in dests:
        row_copy(j, me, 1).start()
    own_grads = pltpu.make_async_copy(
        grads_out.at[pl.ds(pl.multiple_of(me * cap, 16), cap)],
        grads_in.at[pl.ds(pl.multiple_of(me * cap, 16), cap)],
        local_sem.at[8],
    )
    own_grads.start()
    facts_in[me] = facts_out[me]
    for u in far:
        w_copy(u, u, 0).wait_recv()
        w_forward(u, 0, half).start()

    def lines_of(ref, row):
        lines = []
        for g in range(n_dp // per):
            line = ref[g * per, row : row + 1, :]
            for k in range(1, per):
                line = line + ref[g * per + k, row : row + 1, :]
            lines.append(line)
        return jnp.concatenate(lines, axis=1)

    for i in sources:
        slot_copy(i, i).wait_recv()
    landed = lax.broadcasted_iota(jnp.int32, (rows, total_slots), 0) == lines_of(slots_in, 0) - 1
    landing = jnp.where(landed, 1.0, 0.0).astype(bf16)

    def at_home(row):
        return jnp.sum(jnp.where(landed, lines_of(facts_in, row), 0.0), axis=1, keepdims=True)

    own_grads.wait()
    for i in sources:
        back_copy(i, i).wait_recv()
    grads[t] = jnp.dot(landing, grads_in[...], preferred_element_type=f32).astype(bf16)
    for u in peers:
        grad_copy(u, t).start()
    for i in sources:
        fact_copy(i, i).wait_recv()
    sums[t] = jnp.zeros(sums.shape[1:], f32)
    sums[t, 0:1, :] = to_row(at_home(2))
    sums[t, 1:2, :] = to_row(at_home(3))
    for u in peers:
        sum_copy(u, t).start()
    mean_col, scale = at_home(0), at_home(1)
    for u in far:
        w_copy(u, u, 1).wait_recv()
        w_forward(u, 1, half).start()
    for u in peers:
        sum_copy(u, u).wait_recv()
    both = sums[0]
    for u in range(1, n_t):
        both = both + sums[u]
    mean_grad = to_col(both[0:1, :]) / depth
    mean_unit = to_col(both[1:2, :]) / depth * scale
    for u in peers:
        grad_copy(u, u).wait_recv()
    near_copy(near).wait_recv()
    for q in range(2):
        for u in far:
            w_forward(u, q, 1 - half).wait_recv()
    own_rows.wait()
    for k in range(2):
        for i in sources:
            row_copy(i, i, k).wait_recv()
    for c in range(0, cols, chunk):
        piece = rows_by_cols(grads[0], weights[0, c : c + chunk, :])
        for u in range(1, n_t):
            piece = piece + rows_by_cols(grads[u], weights[u, c : c + chunk, :])
        piece = piece * gain_ref[:, pl.ds(pl.multiple_of(t * cols + c, LANES), chunk)]
        away = jnp.dot(landing, arrived[:, c : c + chunk], preferred_element_type=f32) - mean_col
        out_ref[:, c : c + chunk] = (scale * (piece - mean_grad - away * mean_unit)).astype(bf16)

    for u in across_peers + [near]:
        x_copy(u, t).wait_send()
    for u in across_peers:
        x_forward(u).wait_send()
    near_copy(t).wait_send()
    for u in far:
        for q in range(2):
            w_copy(u, t, q).wait_send()
            w_forward(u, q, half).wait_send()
    for u in peers:
        grad_copy(u, t).wait_send()
        sum_copy(u, t).wait_send()
    for j in dests:
        slot_copy(j, me).wait_send()
        fact_copy(j, me).wait_send()
        back_copy(j, me).wait_send()
        for k in range(2):
            row_copy(j, me, k).wait_send()


def per_device(inputs, upstream, proj_weight, proj_bias, norm_gain, home_rows):
    n_dp, n_t = lax.axis_size("dp"), lax.axis_size("tensor")
    rows, cols = inputs.shape
    head = upstream.shape[1]
    cap = max(2, 2 * rows // n_dp)
    dma = pltpu.SemaphoreType.DMA
    in_vmem = pl.BlockSpec(memory_space=pltpu.VMEM)
    return pl.pallas_call(
        functools.partial(kernel, n_dp, n_t, cap),
        out_shape=jax.ShapeDtypeStruct((rows, cols), bf16),
        in_specs=[pl.BlockSpec(memory_space=pltpu.HBM)] * 6,
        out_specs=in_vmem,
        scratch_shapes=[
            pltpu.VMEM((n_t, rows, cols), bf16),
            pltpu.VMEM((rows, head), bf16),
            pltpu.VMEM((1, head), f32),
            pltpu.VMEM((1, n_t * cols), f32),
            pltpu.VMEM((1, rows), jnp.int32),
            pltpu.VMEM((n_t * cols, head), bf16),
            pltpu.VMEM((n_t, cols, head), bf16),
            pltpu.VMEM((n_dp * cap, cols), bf16),
            pltpu.VMEM((n_dp * cap, cols), bf16),
            pltpu.VMEM((n_dp, 8, LANES), jnp.int32),
            pltpu.VMEM((n_dp, 8, LANES), jnp.int32),
            pltpu.VMEM((n_dp, 8, LANES), f32),
            pltpu.VMEM((n_dp, 8, LANES), f32),
            pltpu.VMEM((rows, cols), bf16),
            pltpu.VMEM((n_dp * cap, head), bf16),
            pltpu.VMEM((n_dp * cap, head), bf16),
            pltpu.VMEM((n_t, rows, head), bf16),
            pltpu.VMEM((n_t, 8, rows), f32),
        ]
        + [dma((n_t,))] * 3
        + [dma((n_t, 2))] * 4
        + [dma((1,))] * 2
        + [dma((2, n_dp))] * 2
        + [dma((n_dp,))] * 6
        + [dma((n_t,))] * 4
        + [dma((9,))],
        compiler_params=pltpu.CompilerParams(
            collective_id=0, has_side_effects=True, vmem_limit_bytes=64 * 1024 * 1024
        ),
        cost_estimate=pl.CostEstimate(
            flops=8 * rows * cols * head * n_t, bytes_accessed=2 * n_t * cols * head, transcendentals=rows * head
        ),
    )(
        inputs,
        upstream,
        proj_weight,
        proj_bias.reshape(1, head),
        norm_gain.reshape(1, n_t * cols),
        home_rows.reshape(1, rows),
    )


def solution(mesh):
    return jax.shard_map(
        per_device,
        mesh=mesh,
        in_specs=(
            P("dp", "tensor"),
            P("dp", "tensor"),
            P(None, "tensor"),
            P("tensor"),
            P(),
            P("dp"),
        ),
        out_specs=P("dp", "tensor"),
        check_vma=False,
    )
```

time: 65.6 us -> 63.6 us (0.970)
  the two profiles are of different devices: /device:TPU:13 before, /device:TPU:0 now
where the time goes in v3:
time: 63.6 us; the launch traced here: 63.5 us
  Pallas kernels  61.4 us (97%)
  local copies, waits for them, and re-layouts  2.06 us (3%)
    pallas_call x1, Pallas kernels, per_device(): pl.pallas_call(functools.partial(kernel, n_dp, n_t, cap), out_shape=jax.S...  61.4 us
    unnamed x1, local copies, waits for them, and re-layouts  2.06 us

profile of v3, /device:TPU:0, one launch (start us, length us, event | category | flops | bytes accessed | tf_op | source)
XLA Modules:
  0.0 63.5 jit_solution(15565502413285224550)
XLA Ops:
  0.0 61.4 %shard_map.64 = bf16[256,1536]{1,0:T(8,128)(2,1)} custom-call(bf16[256,1536]{1,0:T(8,128)(2,1)} %x_hbm.1, bf16[256,256]{1,0:T(8,128)(2,1)} %up_hbm.1, bf16[6144,256]{1,0:T(8,128)(2,1)} %w_ref.1, f32[1,256]{1,0:T(1,128)} %bitcast.4, f32[1,6144]{1,0:T(1,128)} %bitcast.3, s32[1,256]{1,0:T(1,128)} %bitcast.5), custom_call_target="tpu_custom_call" | custom-call | flops 3221225472 | bytes 3145728 | tf_op jit(solution)/shard_map/pallas_call | solution.py:355
  61.4 2.1 %copy.8 = bf16[256,1536]{1,0:T(8,128)(2,1)} copy(bf16[256,1536]{1,0:T(8,128)(2,1)} %shard_map.64) | data formatting | bytes 1572864

commit v4 on v3

--- a/solution.py
+++ b/solution.py
@@ -41,7 +41,8 @@
     chunk = math.gcd(cols, 256)
     first = 2 * cols // 3 // LANES * LANES
     parts = [(0, first), (first, cols - first)]
-    quarter = cols // 4
+    pieces = 4
+    quarter = cols // (2 * pieces)
 
     def sibling(u):
         return u + 1 - 2 * lax.rem(u, 2)
@@ -135,10 +136,10 @@
         )
 
     def w_span(which, q):
-        return pl.ds(pl.multiple_of((2 * which + q) * quarter, 16), quarter)
+        return pl.ds(pl.multiple_of((pieces * which + q) * quarter, 16), quarter)
 
     def w_copy(u, block, q):
-        start = pl.multiple_of(u * cols + (2 * half + q) * quarter, 16)
+        start = pl.multiple_of(u * cols + (pieces * half + q) * quarter, 16)
         return remote(
             w_ref.at[pl.ds(start, quarter)], weights.at[block, w_span(half, q)],
             w_send.at[u, q], w_recv.at[block, q], {"tensor": u},
@@ -184,6 +185,8 @@
     for j in dests:
         slot_copy(j, me).start()
         row_copy(j, me, 0).start()
+    for j in dests:
+        row_copy(j, me, 1).start()
     near_copy(t).start()
     own_rows = pltpu.make_async_copy(
         packed.at[pl.ds(pl.multiple_of(me * cap, 16), cap)],
@@ -211,7 +214,7 @@
     for u in across_peers:
         x_copy(u, u).wait_recv()
         x_forward(u).start()
-    for q in range(2):
+    for q in range(pieces):
         for u in far:
             w_copy(u, t, q).start()
     x_copy(near, near).wait_recv()
@@ -253,8 +256,6 @@
     for j in dests:
         back_copy(j, me).start()
         fact_copy(j, me).start()
-    for j in dests:
-        row_copy(j, me, 1).start()
     own_grads = pltpu.make_async_copy(
         grads_out.at[pl.ds(pl.multiple_of(me * cap, 16), cap)],
         grads_in.at[pl.ds(pl.multiple_of(me * cap, 16), cap)],
@@ -262,9 +263,13 @@
     )
     own_grads.start()
     facts_in[me] = facts_out[me]
-    for u in far:
-        w_copy(u, u, 0).wait_recv()
-        w_forward(u, 0, half).start()
+    def pass_on(q):
+        for u in far:
+            w_copy(u, u, q).wait_recv()
+            w_forward(u, q, half).start()
+
+    pass_on(0)
+    pass_on(1)
 
     def lines_of(ref, row):
         lines = []
@@ -283,6 +288,7 @@
     def at_home(row):
         return jnp.sum(jnp.where(landed, lines_of(facts_in, row), 0.0), axis=1, keepdims=True)
 
+    pass_on(2)
     own_grads.wait()
     for i in sources:
         back_copy(i, i).wait_recv()
@@ -297,9 +303,7 @@
     for u in peers:
         sum_copy(u, t).start()
     mean_col, scale = at_home(0), at_home(1)
-    for u in far:
-        w_copy(u, u, 1).wait_recv()
-        w_forward(u, 1, half).start()
+    pass_on(3)
     for u in peers:
         sum_copy(u, u).wait_recv()
     both = sums[0]
@@ -310,19 +314,23 @@
     for u in peers:
         grad_copy(u, u).wait_recv()
     near_copy(near).wait_recv()
-    for q in range(2):
-        for u in far:
-            w_forward(u, q, 1 - half).wait_recv()
     own_rows.wait()
     for k in range(2):
         for i in sources:
             row_copy(i, i, k).wait_recv()
     for c in range(0, cols, chunk):
+        centred[:, c : c + chunk] = jnp.dot(
+            landing, arrived[:, c : c + chunk], preferred_element_type=f32
+        ).astype(bf16)
+    for q in range(pieces):
+        for u in far:
+            w_forward(u, q, 1 - half).wait_recv()
+    for c in range(0, cols, chunk):
         piece = rows_by_cols(grads[0], weights[0, c : c + chunk, :])
         for u in range(1, n_t):
             piece = piece + rows_by_cols(grads[u], weights[u, c : c + chunk, :])
         piece = piece * gain_ref[:, pl.ds(pl.multiple_of(t * cols + c, LANES), chunk)]
-        away = jnp.dot(landing, arrived[:, c : c + chunk], preferred_element_type=f32) - mean_col
+        away = centred[:, c : c + chunk].astype(f32) - mean_col
         out_ref[:, c : c + chunk] = (scale * (piece - mean_grad - away * mean_unit)).astype(bf16)
 
     for u in across_peers + [near]:
@@ -331,7 +339,7 @@
         x_forward(u).wait_send()
     near_copy(t).wait_send()
     for u in far:
-        for q in range(2):
+        for q in range(pieces):
             w_copy(u, t, q).wait_send()
             w_forward(u, q, half).wait_send()
     for u in peers:
@@ -378,14 +386,14 @@
             pltpu.VMEM((n_t, 8, rows), f32),
         ]
         + [dma((n_t,))] * 3
-        + [dma((n_t, 2))] * 4
+        + [dma((n_t, 4))] * 4
         + [dma((1,))] * 2
         + [dma((2, n_dp))] * 2
         + [dma((n_dp,))] * 6
         + [dma((n_t,))] * 4
         + [dma((9,))],
         compiler_params=pltpu.CompilerParams(
-            collective_id=0, has_side_effects=True, vmem_limit_bytes=64 * 1024 * 1024
+            collective_id=0, has_side_effects=True, vmem_limit_bytes=63 * 1024 * 1024
         ),
         cost_estimate=pl.CostEstimate(
             flops=8 * rows * cols * head * n_t, bytes_accessed=2 * n_t * cols * head, transcendentals=rows * head

time: 63.6 us -> 60.8 us (0.956)
  Pallas kernels: 61.4 us -> 58.6 us
    pallas_call x1, Pallas kernels: 61.4 us -> 58.6 us  [per_device(): pl.pallas_call(functools.partial(kernel, n_dp, n_t, cap), out_shape=jax.S...]
where the time goes in v4:
time: 60.8 us; the launch traced here: 60.7 us
  Pallas kernels  58.6 us (96%)
  local copies, waits for them, and re-layouts  2.06 us (3%)
    pallas_call x1, Pallas kernels, per_device(): pl.pallas_call(functools.partial(kernel, n_dp, n_t, cap), out_shape=jax.S...  58.6 us
    unnamed x1, local copies, waits for them, and re-layouts  2.06 us

profile of v4, /device:TPU:0, one launch (start us, length us, event | category | flops | bytes accessed | tf_op | source)
XLA Modules:
  0.0 60.7 jit_solution(17394196666843437160)
XLA Ops:
  0.0 58.6 %shard_map.64 = bf16[256,1536]{1,0:T(8,128)(2,1)} custom-call(bf16[256,1536]{1,0:T(8,128)(2,1)} %x_hbm.1, bf16[256,256]{1,0:T(8,128)(2,1)} %up_hbm.1, bf16[6144,256]{1,0:T(8,128)(2,1)} %w_ref.1, f32[1,256]{1,0:T(1,128)} %bitcast.4, f32[1,6144]{1,0:T(1,128)} %bitcast.3, s32[1,256]{1,0:T(1,128)} %bitcast.5), custom_call_target="tpu_custom_call" | custom-call | flops 3221225472 | bytes 3145728 | tf_op jit(solution)/shard_map/pallas_call | solution.py:363
  58.6 2.1 %copy.8 = bf16[256,1536]{1,0:T(8,128)(2,1)} copy(bf16[256,1536]{1,0:T(8,128)(2,1)} %shard_map.64) | data formatting | bytes 1572864
